TPU v7x, 32 devices: a whole 2x2x4 slice. The times are simulated.
32 devices in a mesh: slab: 2 (over x), pair: 8 (over z, y), quad: 2 (over core).
Axes of the slice: x: 2, y: 2, z: 4, core: 2. Of those that a mesh axis runs over, the one named last changes fastest.
Arguments:
- interferograms: float32 [64, 512, 1024], P(('pair', 'quad'), 'slab'), parts along dimension 1, may hold values from -24 to 24
- pair_epochs: int32 [2, 64], replicated, may hold values from 0 to 31, as said below
- days: int32 [32], replicated, may hold values from 0 to 732, as said below
Outputs:
- smoothed: float32 [32, 512, 1024], P(None, ('slab', 'pair'), 'quad'), parts along dimension 1
There are 2 independent parts, one for each index of `slab`. A program takes and returns all parts, laid end to end along the dimension named above; an argument that names none is the same for every part. Nothing has to cross between parts.
Inputs may be any that keep to these rules, and one draw needn't show every extreme that they name: pair_epochs[0, p] < pair_epochs[1, p] for every pair, the difference is at most 8, and every two consecutive epochs e, e + 1 form one of the pairs. days are strictly increasing, days[0] = 0, consecutive days differ by 12, 24 or 36, and the last day is always the maximum.
All inputs are finite; a program needn't handle non-finite values.
Results may differ from a plain program's by a relative error of at most 0.000071.
Values sent between devices are 32-bit elements; how exact they have to be, the bound alone decides.
A program may use at most 64 MiB of HBM per device.

v0:
```python
import functools
import math

import jax
import jax.numpy as jnp
from jax import lax
from jax.experimental import pallas as pl
from jax.experimental.pallas import tpu as pltpu
from jax.sharding import PartitionSpec as P

E = 32
RADIUS = 6
STRIP = 8
LANES = 128
MESH = pl.DeviceIdType.MESH
HIGHEST = lax.Precision.HIGHEST


def gauss_taps():
    weights = [math.exp(-i * i / 8.0) for i in range(-RADIUS, RADIUS + 1)]
    return [w / sum(weights) for w in weights]


def iota(shape, dim):
    return lax.broadcasted_iota(jnp.int32, shape, dim)


def smooth_rows(column, at_row):
    taps = gauss_taps()
    rows = [column[pl.ds(at_row + STRIP - RADIUS + i, STRIP), :] for i in range(2 * RADIUS + 1)]
    total = taps[RADIUS] * rows[RADIUS]
    for i in range(1, RADIUS + 1):
        total = total + taps[RADIUS + i] * (rows[RADIUS - i] + rows[RADIUS + i])
    return total


def smooth_columns(columns):
    taps = gauss_taps()
    wide = jnp.concatenate(columns + [jnp.zeros_like(columns[0])], axis=1)
    span = wide.shape[1]
    total = taps[RADIUS] * wide
    for i in range(1, RADIUS + 1):
        total = total + taps[RADIUS + i] * (pltpu.roll(wide, i, 1) + pltpu.roll(wide, span - i, 1))
    return total[:, : span - LANES]


def pick(step, table):
    return sum(jnp.where(step == k, value, 0) for k, value in enumerate(table))


def visits(n_outer, n_inner):
    far = sorted(range(n_outer), key=lambda d: -min(d, n_outer - d))
    straight = [(d, 0) for d in far if d]
    bent = [(d, i) for i in range(1, n_inner) for d in reversed(far)]
    order = []
    while straight or bent:
        order += straight[:1] + bent[:1]
        straight, bent = straight[1:], bent[1:]
    return order + [(0, 0)]


def epoch_weights(pair_epochs, days):
    pairs = pair_epochs.shape[1]
    first, second = pair_epochs[0:1], pair_epochs[1:2]
    step = iota((E, pairs), 0)
    design_t = jnp.where((first <= step) & (step < second), 1.0, 0.0)
    row, col = iota((LANES, pairs), 0), iota((LANES, pairs), 1)
    inside = (row < E) & (first <= row) & (row < second)
    other = jnp.where(inside | (row == col + E), 1.0, 0.0)
    system = lax.dot_general(
        design_t, other, (((1,), (1,)), ((), ())), precision=HIGHEST, preferred_element_type=jnp.float32
    )
    row, col = iota((E, LANES), 0), iota((E, LANES), 1)
    system = system + jnp.where((row == E - 1) & (col == E - 1), 1.0, 0.0)

    def eliminate(k, a):
        pivot_row = jnp.sum(jnp.where(row == k, a, 0.0), axis=0, keepdims=True)
        pivot_col = jnp.sum(jnp.where(col == k, a, 0.0), axis=1, keepdims=True)
        pivot = jnp.sum(jnp.where(col[0:1] == k, pivot_row, 0.0), axis=1, keepdims=True)
        scaled = pivot_row / pivot
        return jnp.where(row == k, scaled, a - pivot_col * scaled)

    system = lax.fori_loop(0, E, eliminate, system)

    times = days.astype(jnp.float32)
    centred = (times - jnp.sum(times, axis=1, keepdims=True) / E) / 365.25
    phase = 2.0 * math.pi * times / 365.25
    erow, ecol = iota((E, E), 0), iota((E, E), 1)
    rest = jnp.where(erow == ecol, 1.0, 0.0)
    basis = []
    for column in (jnp.ones_like(times), centred, jnp.sin(phase), jnp.cos(phase)):
        for _ in range(2):
            for q in basis:
                column = column - q * jnp.sum(q * column, axis=1, keepdims=True)
        column = column / jnp.sqrt(jnp.sum(column * column, axis=1, keepdims=True))
        basis.append(column)
        upright = jnp.sum(jnp.where(erow == ecol, column, 0.0), axis=1, keepdims=True)
        rest = rest - upright * column
    summing = jnp.where(ecol < erow, 1.0, 0.0)
    displacement = jnp.dot(summing, system, precision=HIGHEST, preferred_element_type=jnp.float32)
    return jnp.dot(rest, displacement, precision=HIGHEST, preferred_element_type=jnp.float32)


def spread_weights(weights, pairs):
    tall, wide = E * STRIP, pairs * STRIP
    right = jnp.where(iota((LANES, wide), 0) == iota((LANES, wide), 1) // STRIP + E, 1.0, 0.0)
    left = jnp.where(iota((tall, E), 1) == iota((tall, E), 0) // STRIP, 1.0, 0.0)
    full = jnp.dot(weights, right, precision=HIGHEST, preferred_element_type=jnp.float32)
    full = jnp.dot(left, full, precision=HIGHEST, preferred_element_type=jnp.float32)
    same = iota((tall, wide), 0) % STRIP == iota((tall, wide), 1) % STRIP
    return jnp.where(same, full, 0.0)


def kernel(n_pair, n_quad, n_inner, x_hbm, epochs_hbm, days_hbm, out_hbm, padded, ready, held, spread, result, epochs_ref, days_ref, in_sem, small_sem, send_sem, recv_sem, out_sem):
    local, height, width = ready.shape
    n = n_pair * n_quad
    rows, cols = height // n_pair, width // n_quad
    strips = rows // STRIP
    slab = lax.axis_index("slab")
    my_pair = lax.axis_index("pair")
    my_quad = lax.axis_index("quad")
    me = my_pair * n_quad + my_quad

    tiles = width // LANES
    loads = [
        pltpu.make_async_copy(
            x_hbm.at[l, :, pl.ds(j * LANES, LANES)],
            padded.at[l, j, pl.ds(STRIP, height), :],
            in_sem.at[l, j],
        )
        for l in range(local)
        for j in range(tiles)
    ]
    loads += [
        pltpu.make_async_copy(epochs_hbm, epochs_ref, small_sem.at[0]),
        pltpu.make_async_copy(days_hbm, days_ref, small_sem.at[1]),
    ]
    for load in loads:
        load.start()
    barrier = pltpu.get_barrier_semaphore()

    def greet(j, carry):
        other = lax.rem(me + j, n)
        pl.semaphore_signal(
            barrier, inc=1, device_id=(slab, other // n_quad, other % n_quad), device_id_type=MESH
        )
        return carry

    lax.fori_loop(1, n, greet, 0)
    edge = jnp.zeros((local, tiles, STRIP, LANES), jnp.float32)
    padded[:, :, 0:STRIP, :] = edge
    padded[:, :, STRIP + height : 2 * STRIP + height, :] = edge
    for load in loads:
        load.wait()
    pl.semaphore_wait(barrier, n - 1)

    def part(t, pair, quad):
        at_row = pl.multiple_of(pair * rows + t * STRIP, STRIP)
        at_col = pl.multiple_of(quad * cols, LANES)
        return ready.at[:, pl.ds(at_row, STRIP), pl.ds(at_col, cols)]

    def slot(t, source):
        return held.at[source, :, pl.ds(pl.multiple_of(t * STRIP, STRIP), STRIP), :]

    def send(t, pair, quad):
        return pltpu.make_async_remote_copy(
            src_ref=part(t, pair, quad),
            dst_ref=slot(t, me),
            send_sem=send_sem.at[t, pair * n_quad + quad],
            recv_sem=recv_sem.at[t, me],
            device_id=(slab, pair, quad),
            device_id_type=MESH,
        )

    n_outer = n_pair // n_inner
    order = visits(n_outer, n_inner)

    def produce(i, carry):
        t, s = i // n_pair, i % n_pair
        outer = (my_pair // n_inner + pick(s, [o for o, _ in order])) % n_outer
        inner = (my_pair % n_inner + pick(s, [i for _, i in order])) % n_inner
        pair = outer * n_inner + inner
        at_row = pl.multiple_of(pair * rows + t * STRIP, STRIP)
        for l in range(local):
            columns = [smooth_rows(padded.at[l, j], at_row) for j in range(tiles)]
            ready[l, pl.ds(at_row, STRIP), :] = smooth_columns(columns)
        for j in range(1, n_quad):
            send(t, pair, (my_quad + j) % n_quad).start()

        @pl.when(pair != my_pair)
        def _():
            send(t, pair, my_quad).start()

        @pl.when(pair == my_pair)
        def _():
            pltpu.make_async_copy(part(t, my_pair, my_quad), slot(t, me), recv_sem.at[t, me]).start()

        return carry

    lax.fori_loop(0, strips * n_pair, produce, 0)

    spread[...] = spread_weights(epoch_weights(epochs_ref[...], days_ref[...]), local * n)

    def out_copy(t):
        at = pl.ds(pl.multiple_of(t * STRIP, STRIP), STRIP)
        return pltpu.make_async_copy(result.at[:, at, :], out_hbm.at[:, at, :], out_sem.at[t])

    def consume(t, carry):
        def arrived(source, carry):
            pltpu.make_async_copy(slot(t, source), slot(t, source), recv_sem.at[t, source]).wait()
            return carry

        lax.fori_loop(0, n, arrived, 0)
        at = pl.ds(pl.multiple_of(t * STRIP, STRIP), STRIP)
        stack = held[:, :, at, :].reshape(n * local * STRIP, cols)
        total = jnp.dot(spread[...], stack, precision=HIGHEST, preferred_element_type=jnp.float32)
        result[:, at, :] = total.reshape(E, STRIP, cols)
        out_copy(t).start()
        return carry

    lax.fori_loop(0, strips, consume, 0)

    def sent(i, carry):
        t, other = i // (n - 1), lax.rem(me + 1 + i % (n - 1), n)
        send(t, other // n_quad, other % n_quad).wait_send()
        return carry

    lax.fori_loop(0, strips * (n - 1), sent, 0)
    for t in range(strips):
        out_copy(t).wait()


def shards(n_inner, interferograms, pair_epochs, days):
    n_pair = lax.axis_size("pair")
    n_quad = lax.axis_size("quad")
    n = n_pair * n_quad
    local, height, width = interferograms.shape
    rows, cols = height // n_pair, width // n_quad
    strips = rows // STRIP
    pairs = local * n
    return pl.pallas_call(
        functools.partial(kernel, n_pair, n_quad, n_inner),
        out_shape=jax.ShapeDtypeStruct((E, rows, cols), jnp.float32),
        in_specs=[pl.BlockSpec(memory_space=pl.ANY)] * 3,
        out_specs=pl.BlockSpec(memory_space=pl.ANY),
        scratch_shapes=[
            pltpu.VMEM((local, width // LANES, height + 2 * STRIP, LANES), jnp.float32),
            pltpu.VMEM((local, height, width), jnp.float32),
            pltpu.VMEM((n, local, rows, cols), jnp.float32),
            pltpu.VMEM((E * STRIP, pairs * STRIP), jnp.float32),
            pltpu.VMEM((E, rows, cols), jnp.float32),
            pltpu.VMEM(pair_epochs.shape, jnp.int32),
            pltpu.VMEM((1,) + days.shape, jnp.int32),
            pltpu.SemaphoreType.DMA((local, width // LANES)),
            pltpu.SemaphoreType.DMA((2,)),
            pltpu.SemaphoreType.DMA((strips, n)),
            pltpu.SemaphoreType.DMA((strips, n)),
            pltpu.SemaphoreType.DMA((strips,)),
        ],
        compiler_params=pltpu.CompilerParams(
            collective_id=0, has_side_effects=True, vmem_limit_bytes=48 * 1024 * 1024
        ),
        name="smooth_and_invert",
    )(interferograms, pair_epochs, days[None, :])


def inner_size(mesh):
    line = list(mesh.devices[0, :, 0])
    coords = [getattr(d, "coords", None) for d in line]
    if any(c is None for c in coords):
        return 1
    moving = [k for k in range(len(coords[0])) if coords[0][k] != coords[-1][k]]
    for k in moving:
        run = 1
        while run < len(line) and coords[run][k] == coords[0][k]:
            run += 1
        if 1 < run < len(line) and len(line) % run == 0:
            return run
    return 1


def solution(mesh):
    placed = (P(("pair", "quad"), "slab", None), P(), P())
    return jax.shard_map(
        functools.partial(shards, inner_size(mesh)),
        mesh=mesh,
        in_specs=placed,
        out_specs=P(None, ("slab", "pair"), "quad"),
        check_vma=False,
    )
```

profile of v0, /device:TPU:0, one launch (start us, length us, event | category | flops | bytes accessed | tf_op | source)
XLA Modules:
  0.0 105.3 jit_solution(17904040849207143900)
XLA Ops:
  0.0 0.0 copy-start
  0.0 0.7 copy-done
  0.7 0.0 copy-start.1
  0.7 0.7 copy-done.1
  1.3 102.6 %smooth_and_invert.1 = f32[32,32,512]{2,1,0:T(8,128)S(1)} custom-call(f32[4,256,1024]{2,1,0:T(8,128)} %x_hbm.1, s32[2,64]{1,0:T(2,128)S(1)} %copy-done, s32[1,32]{1,0:T(1,128)S(1)} %bitcast.1), custom_call_target="tpu_custom_call" | custom-call | tf_op jit(solution)/shard_map/smooth_and_invert/pallas_call | solution.py:241
  104.0 1.3 %copy.5 = f32[32,32,512]{2,1,0:T(8,128)} copy(f32[32,32,512]{2,1,0:T(8,128)S(1)} %smooth_and_invert.1) | data formatting | bytes 4194304
Async XLA Ops:
  0.0 0.7 copy-start
  0.7 0.7 copy-start.1
where the time goes:
time: 105 us
  Pallas kernels  103 us (98%)
  local copies, waits for them, and re-layouts  2.65 us (3%)
    pallas_call x1, Pallas kernels, shards(): pl.pallas_call(functools.partial(kernel, n_pair, n_quad, n_inner), out_sh...  103 us
    unnamed x5, local copies, waits for them, and re-layouts  2.65 us

commit v1 on v0

--- a/solution.py
+++ b/solution.py
@@ -14,6 +14,7 @@
 LANES = 128
 MESH = pl.DeviceIdType.MESH
 HIGHEST = lax.Precision.HIGHEST
+TERMS = 4
 
 
 def gauss_taps():
@@ -44,22 +45,7 @@
     return total[:, : span - LANES]
 
 
-def pick(step, table):
-    return sum(jnp.where(step == k, value, 0) for k, value in enumerate(table))
-
-
-def visits(n_outer, n_inner):
-    far = sorted(range(n_outer), key=lambda d: -min(d, n_outer - d))
-    straight = [(d, 0) for d in far if d]
-    bent = [(d, i) for i in range(1, n_inner) for d in reversed(far)]
-    order = []
-    while straight or bent:
-        order += straight[:1] + bent[:1]
-        straight, bent = straight[1:], bent[1:]
-    return order + [(0, 0)]
-
-
-def epoch_weights(pair_epochs, days):
+def pair_weights(pair_epochs, days):
     pairs = pair_epochs.shape[1]
     first, second = pair_epochs[0:1], pair_epochs[1:2]
     step = iota((E, pairs), 0)
@@ -86,24 +72,30 @@
     centred = (times - jnp.sum(times, axis=1, keepdims=True) / E) / 365.25
     phase = 2.0 * math.pi * times / 365.25
     erow, ecol = iota((E, E), 0), iota((E, E), 1)
-    rest = jnp.where(erow == ecol, 1.0, 0.0)
-    basis = []
-    for column in (jnp.ones_like(times), centred, jnp.sin(phase), jnp.cos(phase)):
-        for _ in range(2):
-            for q in basis:
-                column = column - q * jnp.sum(q * column, axis=1, keepdims=True)
-        column = column / jnp.sqrt(jnp.sum(column * column, axis=1, keepdims=True))
-        basis.append(column)
-        upright = jnp.sum(jnp.where(erow == ecol, column, 0.0), axis=1, keepdims=True)
-        rest = rest - upright * column
+    lane = ecol[0:1]
+    eye = jnp.where(erow == ecol, 1.0, 0.0)
+    q, q_t = eye, eye
+    columns = [jnp.ones_like(times), centred, jnp.sin(phase), jnp.cos(phase)]
+    for j in range(TERMS):
+        below = jnp.where(lane >= j, columns[j], 0.0)
+        head = jnp.sum(jnp.where(lane == j, below, 0.0), axis=1, keepdims=True)
+        norm = jnp.sqrt(jnp.sum(below * below, axis=1, keepdims=True))
+        v = below + jnp.where(lane == j, jnp.where(head >= 0, norm, -norm), 0.0)
+        v = v * lax.rsqrt(0.5 * jnp.sum(v * v, axis=1, keepdims=True))
+        upright = jnp.sum(jnp.where(erow == ecol, v, 0.0), axis=1, keepdims=True)
+        columns = [c - v * jnp.sum(v * c, axis=1, keepdims=True) for c in columns]
+        q = q - jnp.sum(q * v, axis=1, keepdims=True) * v
+        q_t = q_t - upright * jnp.sum(q_t * upright, axis=0, keepdims=True)
+    q = jnp.where(ecol >= TERMS, q, 0.0)
+    q_t = jnp.where(erow >= TERMS, q_t, 0.0)
     summing = jnp.where(ecol < erow, 1.0, 0.0)
     displacement = jnp.dot(summing, system, precision=HIGHEST, preferred_element_type=jnp.float32)
-    return jnp.dot(rest, displacement, precision=HIGHEST, preferred_element_type=jnp.float32)
-
-
-def spread_weights(weights, pairs):
-    tall, wide = E * STRIP, pairs * STRIP
-    right = jnp.where(iota((LANES, wide), 0) == iota((LANES, wide), 1) // STRIP + E, 1.0, 0.0)
+    return q, jnp.dot(q_t, displacement, precision=HIGHEST, preferred_element_type=jnp.float32)
+
+
+def spread_weights(weights, first, count):
+    tall, wide, depth = E * STRIP, count * STRIP, weights.shape[1]
+    right = jnp.where(iota((depth, wide), 0) == iota((depth, wide), 1) // STRIP + first, 1.0, 0.0)
     left = jnp.where(iota((tall, E), 1) == iota((tall, E), 0) // STRIP, 1.0, 0.0)
     full = jnp.dot(weights, right, precision=HIGHEST, preferred_element_type=jnp.float32)
     full = jnp.dot(left, full, precision=HIGHEST, preferred_element_type=jnp.float32)
@@ -111,17 +103,40 @@
     return jnp.where(same, full, 0.0)
 
 
-def kernel(n_pair, n_quad, n_inner, x_hbm, epochs_hbm, days_hbm, out_hbm, padded, ready, held, spread, result, epochs_ref, days_ref, in_sem, small_sem, send_sem, recv_sem, out_sem):
+def times_stack(weights, stack):
+    flat = stack.reshape(weights.shape[1], stack.shape[-1])
+    total = jnp.dot(weights, flat, precision=HIGHEST, preferred_element_type=jnp.float32)
+    return total.reshape(E, STRIP, stack.shape[-1])
+
+
+def raw_strips(n_outer, strips):
+    return 1 if n_outer > 1 and n_outer // 2 <= 2 else strips
+
+
+def kernel(
+    n_pair, n_quad, n_inner,
+    x_hbm, epochs_hbm, days_hbm, out_hbm,
+    padded, ready, held, gathered, summed, arrived, spread, result, epochs_ref, days_ref,
+    in_sem, small_sem, send_sem, recv_sem, gather_sem, sum_send_sem, sum_recv_sem, out_sem,
+):
     local, height, width = ready.shape
     n = n_pair * n_quad
+    n_outer = n_pair // n_inner
+    half_n, half_pair = n // 2, n_pair // 2
+    far = n_outer // 2
     rows, cols = height // n_pair, width // n_quad
     strips = rows // STRIP
+    raw = raw_strips(n_outer, strips)
+    tiles = width // LANES
     slab = lax.axis_index("slab")
     my_pair = lax.axis_index("pair")
     my_quad = lax.axis_index("quad")
     me = my_pair * n_quad + my_quad
-
-    tiles = width // LANES
+    side = my_pair // half_pair
+    my_source = me % half_n
+    my_inner = my_pair % n_inner
+    edge_outer = far - 1 + side
+
     loads = [
         pltpu.make_async_copy(
             x_hbm.at[l, :, pl.ds(j * LANES, LANES)],
@@ -150,9 +165,14 @@
     edge = jnp.zeros((local, tiles, STRIP, LANES), jnp.float32)
     padded[:, :, 0:STRIP, :] = edge
     padded[:, :, STRIP + height : 2 * STRIP + height, :] = edge
+    if raw < strips:
+        arrived[0:TERMS] = jnp.zeros((TERMS, rows, cols), jnp.float32)
     for load in loads:
         load.wait()
     pl.semaphore_wait(barrier, n - 1)
+
+    def strip_rows(t):
+        return pl.ds(pl.multiple_of(t * STRIP, STRIP), STRIP)
 
     def part(t, pair, quad):
         at_row = pl.multiple_of(pair * rows + t * STRIP, STRIP)
@@ -160,7 +180,10 @@
         return ready.at[:, pl.ds(at_row, STRIP), pl.ds(at_col, cols)]
 
     def slot(t, source):
-        return held.at[source, :, pl.ds(pl.multiple_of(t * STRIP, STRIP), STRIP), :]
+        return held.at[source, :, strip_rows(t), :]
+
+    def gather_slot(t, at, source):
+        return gathered.at[at, source, :, strip_rows(t), :]
 
     def send(t, pair, quad):
         return pltpu.make_async_remote_copy(
@@ -172,18 +195,60 @@
             device_id_type=MESH,
         )
 
-    n_outer = n_pair // n_inner
-    order = visits(n_outer, n_inner)
-
-    def produce(i, carry):
-        t, s = i // n_pair, i % n_pair
-        outer = (my_pair // n_inner + pick(s, [o for o, _ in order])) % n_outer
-        inner = (my_pair % n_inner + pick(s, [i for _, i in order])) % n_inner
-        pair = outer * n_inner + inner
+    def place(pair):
+        return pair // n_inner - (1 - side) * far, edge_outer * n_inner + pair % n_inner
+
+    def send_to_sum(t, pair, quad):
+        at, target = place(pair)
+        return pltpu.make_async_remote_copy(
+            src_ref=part(t, pair, quad),
+            dst_ref=gather_slot(t, at, my_source),
+            send_sem=send_sem.at[t, pair * n_quad + quad],
+            recv_sem=gather_sem.at[t, at, my_source],
+            device_id=(slab, target, quad),
+            device_id_type=MESH,
+        )
+
+    def smooth(t, pair):
         at_row = pl.multiple_of(pair * rows + t * STRIP, STRIP)
         for l in range(local):
             columns = [smooth_rows(padded.at[l, j], at_row) for j in range(tiles)]
             ready[l, pl.ds(at_row, STRIP), :] = smooth_columns(columns)
+
+    def across(s):
+        outer, inner = s // n_inner, (s + my_inner) % n_inner
+        return ((1 - side) * (2 * far - 1 - outer) + side * outer) * n_inner + inner
+
+    def produce_raw(i, carry):
+        t, pair = i // half_pair, across(i % half_pair)
+        smooth(t, pair)
+        for j in range(n_quad):
+            send(t, pair, (my_quad + j) % n_quad).start()
+        return carry
+
+    def produce_summed(i, carry):
+        t, pair = raw + i // half_pair, across(i % half_pair)
+        smooth(t, pair)
+        at, target = place(pair)
+        for j in range(1, n_quad):
+            send_to_sum(t, pair, (my_quad + j) % n_quad).start()
+
+        @pl.when(target != my_pair)
+        def _():
+            send_to_sum(t, pair, my_quad).start()
+
+        @pl.when(target == my_pair)
+        def _():
+            pltpu.make_async_copy(
+                part(t, pair, my_quad), gather_slot(t, at, my_source), gather_sem.at[t, at, my_source]
+            ).start()
+
+        return carry
+
+    def produce_near(i, carry):
+        t, s = i // half_pair, i % half_pair
+        pair = side * half_pair + (my_pair + 1 + s) % half_pair
+        smooth(t, pair)
         for j in range(1, n_quad):
             send(t, pair, (my_quad + j) % n_quad).start()
 
@@ -197,35 +262,124 @@
 
         return carry
 
-    lax.fori_loop(0, strips * n_pair, produce, 0)
-
-    spread[...] = spread_weights(epoch_weights(epochs_ref[...], days_ref[...]), local * n)
-
-    def out_copy(t):
-        at = pl.ds(pl.multiple_of(t * STRIP, STRIP), STRIP)
-        return pltpu.make_async_copy(result.at[:, at, :], out_hbm.at[:, at, :], out_sem.at[t])
-
-    def consume(t, carry):
-        def arrived(source, carry):
+    def sum_copy(t, at):
+        return pltpu.make_async_remote_copy(
+            src_ref=summed.at[at, pl.ds(TERMS, E - TERMS), strip_rows(t), :],
+            dst_ref=arrived.at[pl.ds(TERMS, E - TERMS), strip_rows(t), :],
+            send_sem=sum_send_sem.at[t, at],
+            recv_sem=sum_recv_sem.at[t],
+            device_id=(slab, ((1 - side) * far + at) * n_inner + my_inner, my_quad),
+            device_id_type=MESH,
+        )
+
+    def add_up(i, carry):
+        t, k = i // far, i % far
+        at = (far - 1 - k) * (1 - side) + k * side
+
+        def wait(source, carry):
+            pltpu.make_async_copy(
+                gather_slot(t, at, source), gather_slot(t, at, source), gather_sem.at[t, at, source]
+            ).wait()
+            return carry
+
+        lax.fori_loop(0, half_n, wait, 0)
+        summed[at, :, strip_rows(t), :] = times_stack(spread[2], gathered[at, :, :, strip_rows(t), :])
+        sum_copy(t, at).start()
+        return carry
+
+    lax.fori_loop(0, raw * half_pair, produce_raw, 0)
+    if raw < strips:
+        lax.fori_loop(0, (strips - raw) * half_pair, produce_summed, 0)
+
+    q, v = pair_weights(epochs_ref[...], days_ref[...])
+    m = jnp.dot(q, v, precision=HIGHEST, preferred_element_type=jnp.float32)
+    count = half_n * local
+    spread[0] = spread_weights(m, E + side * count, count)
+    spread[1] = spread_weights(m, E + (1 - side) * count, count)
+    if raw < strips:
+        spread[2] = spread_weights(v, E + side * count, count)
+        spread[3] = spread_weights(q, 0, E)
+
+        @pl.when(my_pair // n_inner == edge_outer)
+        def _():
+            lax.fori_loop(raw * far, (raw + 1) * far, add_up, 0)
+
+    lax.fori_loop(0, strips * half_pair, produce_near, 0)
+
+    if raw < strips:
+
+        @pl.when(my_pair // n_inner == edge_outer)
+        def _():
+            lax.fori_loop((raw + 1) * far, strips * far, add_up, 0)
+
+    def wait_for(t, first):
+        def wait(source, carry):
             pltpu.make_async_copy(slot(t, source), slot(t, source), recv_sem.at[t, source]).wait()
             return carry
 
-        lax.fori_loop(0, n, arrived, 0)
-        at = pl.ds(pl.multiple_of(t * STRIP, STRIP), STRIP)
-        stack = held[:, :, at, :].reshape(n * local * STRIP, cols)
-        total = jnp.dot(spread[...], stack, precision=HIGHEST, preferred_element_type=jnp.float32)
-        result[:, at, :] = total.reshape(E, STRIP, cols)
+        lax.fori_loop(first, first + half_n, wait, 0)
+
+    def out_copy(t):
+        return pltpu.make_async_copy(result.at[:, strip_rows(t), :], out_hbm.at[:, strip_rows(t), :], out_sem.at[t])
+
+    def own_side(t, carry):
+        wait_for(t, side * half_n)
+        stack = held[pl.ds(side * half_n, half_n), :, strip_rows(t), :]
+        result[:, strip_rows(t), :] = times_stack(spread[0], stack)
+        return carry
+
+    def far_side(t, carry):
+        wait_for(t, (1 - side) * half_n)
+        stack = held[pl.ds((1 - side) * half_n, half_n), :, strip_rows(t), :]
+        result[:, strip_rows(t), :] += times_stack(spread[1], stack)
         out_copy(t).start()
         return carry
 
-    lax.fori_loop(0, strips, consume, 0)
-
-    def sent(i, carry):
-        t, other = i // (n - 1), lax.rem(me + 1 + i % (n - 1), n)
+    def far_sums(t, carry):
+        strip = arrived.at[pl.ds(TERMS, E - TERMS), strip_rows(t), :]
+        pltpu.make_async_copy(strip, strip, sum_recv_sem.at[t]).wait()
+        result[:, strip_rows(t), :] += times_stack(spread[3], arrived[:, strip_rows(t), :])
+        out_copy(t).start()
+        return carry
+
+    lax.fori_loop(0, strips, own_side, 0)
+    lax.fori_loop(0, raw, far_side, 0)
+    if raw < strips:
+        lax.fori_loop(raw, strips, far_sums, 0)
+
+    def sent_raw(i, carry):
+        t, other = i // half_n, (1 - side) * half_n + i % half_n
         send(t, other // n_quad, other % n_quad).wait_send()
         return carry
 
-    lax.fori_loop(0, strips * (n - 1), sent, 0)
+    def sent_summed(i, carry):
+        t, other = raw + i // half_n, (1 - side) * half_n + i % half_n
+        pair, quad = other // n_quad, other % n_quad
+
+        @pl.when(place(pair)[1] * n_quad + quad != me)
+        def _():
+            send_to_sum(t, pair, quad).wait_send()
+
+        return carry
+
+    def sent_near(i, carry):
+        t, other = i // (half_n - 1), side * half_n + (me + 1 + i % (half_n - 1)) % half_n
+        send(t, other // n_quad, other % n_quad).wait_send()
+        return carry
+
+    def sent_sums(i, carry):
+        sum_copy(i // far, i % far).wait_send()
+        return carry
+
+    lax.fori_loop(0, raw * half_n, sent_raw, 0)
+    lax.fori_loop(0, strips * (half_n - 1), sent_near, 0)
+    if raw < strips:
+        lax.fori_loop(0, (strips - raw) * half_n, sent_summed, 0)
+
+        @pl.when(my_pair // n_inner == edge_outer)
+        def _():
+            lax.fori_loop(raw * far, strips * far, sent_sums, 0)
+
     for t in range(strips):
         out_copy(t).wait()
 
@@ -237,7 +391,10 @@
     local, height, width = interferograms.shape
     rows, cols = height // n_pair, width // n_quad
     strips = rows // STRIP
-    pairs = local * n
+    far = n_pair // n_inner // 2
+    sums = raw_strips(n_pair // n_inner, strips) < strips
+    gathered = (far, n // 2, local, rows, cols) if sums else (1, 1, local, STRIP, LANES)
+    summed = (far, E, rows, cols) if sums else (1, E, STRIP, LANES)
     return pl.pallas_call(
         functools.partial(kernel, n_pair, n_quad, n_inner),
         out_shape=jax.ShapeDtypeStruct((E, rows, cols), jnp.float32),
@@ -247,7 +404,10 @@
             pltpu.VMEM((local, width // LANES, height + 2 * STRIP, LANES), jnp.float32),
             pltpu.VMEM((local, height, width), jnp.float32),
             pltpu.VMEM((n, local, rows, cols), jnp.float32),
-            pltpu.VMEM((E * STRIP, pairs * STRIP), jnp.float32),
+            pltpu.VMEM(gathered, jnp.float32),
+            pltpu.VMEM(summed, jnp.float32),
+            pltpu.VMEM(summed[1:], jnp.float32),
+            pltpu.VMEM((4, E * STRIP, n // 2 * local * STRIP), jnp.float32),
             pltpu.VMEM((E, rows, cols), jnp.float32),
             pltpu.VMEM(pair_epochs.shape, jnp.int32),
             pltpu.VMEM((1,) + days.shape, jnp.int32),
@@ -255,6 +415,9 @@
             pltpu.SemaphoreType.DMA((2,)),
             pltpu.SemaphoreType.DMA((strips, n)),
             pltpu.SemaphoreType.DMA((strips, n)),
+            pltpu.SemaphoreType.DMA((strips, far, n // 2) if sums else (1, 1, 1)),
+            pltpu.SemaphoreType.DMA((strips, far)),
+            pltpu.SemaphoreType.DMA((strips,)),
             pltpu.SemaphoreType.DMA((strips,)),
         ],
         compiler_params=pltpu.CompilerParams(

time: 105 us -> 95.8 us (0.912)
  the two profiles are of different devices: /device:TPU:0 before, /device:TPU:8 now
where the time goes in v1:
time: 95.8 us; the launch traced here: 95.6 us
  Pallas kernels  93 us (97%)
  local copies, waits for them, and re-layouts  2.65 us (3%)
    pallas_call x1, Pallas kernels, shards(): pl.pallas_call(functools.partial(kernel, n_pair, n_quad, n_inner), out_sh...  93 us
    unnamed x5, local copies, waits for them, and re-layouts  2.65 us

profile of v1, /device:TPU:8, one launch (start us, length us, event | category | flops | bytes accessed | tf_op | source)
XLA Modules:
  0.0 95.6 jit_solution(2638277720160666124)
XLA Ops:
  0.0 0.0 copy-start
  0.0 0.7 copy-done
  0.7 0.0 copy-start.1
  0.7 0.7 copy-done.1
  1.3 93.0 %smooth_and_invert.1 = f32[32,32,512]{2,1,0:T(8,128)S(1)} custom-call(f32[4,256,1024]{2,1,0:T(8,128)} %x_hbm.1, s32[2,64]{1,0:T(2,128)S(1)} %copy-done, s32[1,32]{1,0:T(1,128)S(1)} %bitcast.1), custom_call_target="tpu_custom_call" | custom-call | tf_op jit(solution)/shard_map/smooth_and_invert/pallas_call | solution.py:398
  94.3 1.3 %copy.5 = f32[32,32,512]{2,1,0:T(8,128)} copy(f32[32,32,512]{2,1,0:T(8,128)S(1)} %smooth_and_invert.1) | data formatting | bytes 4194304
Async XLA Ops:
  0.0 0.7 copy-start
  0.7 0.7 copy-start.1
